TPU v7x, 32 devices: a whole 2x2x4 slice. The times are simulated.
32 devices in a mesh: seq: 8 (over y, x, core), chan: 4 (over z).
Axes of the slice: x: 2, y: 2, z: 4, core: 2. Of those that a mesh axis runs over, the one named last changes fastest.
Arguments:
- frames: bfloat16 [10, 1536, 4096], P(None, 'chan', 'seq'), may hold values from -6 to 6
- conv_taps: float32 [4, 1536], P(None, 'chan'), may hold values from -3 to 3
- left_factor: bfloat16 [8, 512, 512], P('seq'), may hold values from -0.25 to 0.25
- right_factor: bfloat16 [512, 8, 8], P('seq'), may hold values from -2 to 2
- out_grad: bfloat16 [10, 1536, 4096], P(None, 'chan', 'seq'), may hold values from -6 to 6
Outputs:
- mixed: bfloat16 [10, 1536, 4096], P(None, 'chan', 'seq')
- frames_grad: bfloat16 [10, 1536, 4096], P(None, 'chan', 'seq')
- left_grad: float32 [8, 512, 512], P('seq', 'chan')
- right_grad: float32 [512, 8, 8], P('seq', 'chan')
All inputs are finite; a program needn't handle non-finite values.
Results may differ from a plain program's by a relative error of at most 0.0057.
Values may be sent and summed in bfloat16 or wider, within the bound.
A program may use at most 128 MiB of HBM per device.

v0:
```python
import jax
import jax.numpy as jnp
from jax import lax
from jax.sharding import PartitionSpec as P

TAPS = 4


def from_behind(value, axis, steps):
    count = lax.axis_size(axis)
    leading, last = (max(0, -steps), min(count, count - steps))
    return lax.ppermute(value, axis, [(source, source + steps) for source in range(leading, last)])


def finish_grads(left_part, right_part):
    return (
        lax.psum_scatter(left_part, "chan", scatter_dimension=1, tiled=True),
        lax.psum_scatter(right_part, "chan", scatter_dimension=1, tiled=True),
    )


def shards(frames, conv_taps, left_factor, right_factor, out_grad):
    clips, chans, rows = frames.shape
    nseq = lax.axis_size("seq")
    blocks_here = left_factor.shape[0]
    width = left_factor.shape[1]
    keep = width // nseq
    total_blocks = blocks_here * nseq
    rim = TAPS - 1
    xf = frames.astype(jnp.float32)
    before = from_behind(frames[:, :, rows - rim :], "seq", 1)
    padded = jnp.concatenate([before, frames], axis=2).astype(jnp.float32)
    mixed_conv = jnp.zeros((clips, chans, rows), jnp.float32)
    for step in range(TAPS):
        mixed_conv = (
            mixed_conv
            + conv_taps[step][None, :, None] * padded[:, :, rim - step : rim - step + rows]
        )
    conv = mixed_conv.astype(jnp.bfloat16).reshape(clips, chans, blocks_here, width)
    first = jnp.einsum(
        "cdij,ijk->cdik", conv, left_factor, preferred_element_type=jnp.float32
    ).astype(jnp.bfloat16)
    columns = lax.all_to_all(first, "seq", split_axis=3, concat_axis=2, tiled=True)
    second = jnp.einsum(
        "cdik,kim->cdkm", columns, right_factor, preferred_element_type=jnp.float32
    ).reshape(clips, chans, rows)
    sig = jax.nn.sigmoid(xf)
    gate = xf * sig
    mixed = (second * gate).astype(jnp.bfloat16)
    cotf = out_grad.astype(jnp.float32)
    dsecond = (cotf * gate).astype(jnp.bfloat16).reshape(clips, chans, keep, total_blocks)
    gate_part = cotf * second * sig * (1.0 + xf * (1.0 - sig))
    right_part = jnp.einsum("cdik,cdkm->kim", columns, dsecond, preferred_element_type=jnp.float32)
    dfirst = jnp.einsum(
        "cdkm,kim->cdik", dsecond, right_factor, preferred_element_type=jnp.float32
    ).astype(jnp.bfloat16)
    back_rows = lax.all_to_all(dfirst, "seq", split_axis=2, concat_axis=3, tiled=True)
    left_part = jnp.einsum("cdij,cdik->ijk", conv, back_rows, preferred_element_type=jnp.float32)
    dconv = jnp.einsum(
        "cdik,ijk->cdij", back_rows, left_factor, preferred_element_type=jnp.float32
    ).reshape(clips, chans, rows)
    after = from_behind(dconv[:, :, :rim], "seq", -1)
    extended = jnp.concatenate([dconv, after], axis=2)
    conv_back = jnp.zeros((clips, chans, rows), jnp.float32)
    for step in range(TAPS):
        conv_back = conv_back + conv_taps[step][None, :, None] * extended[:, :, step : step + rows]
    frames_grad = (gate_part + conv_back).astype(jnp.bfloat16)
    grads = finish_grads(left_part, right_part)
    return (mixed, frames_grad, grads[0], grads[1])


def solution(mesh):
    placed = (
        P(None, "chan", "seq"),
        P(None, "chan"),
        P("seq", None, None),
        P("seq", None, None),
        P(None, "chan", "seq"),
    )
    return jax.shard_map(
        shards,
        mesh=mesh,
        in_specs=placed,
        out_specs=(
            P(None, "chan", "seq"),
            P(None, "chan", "seq"),
            P("seq", "chan", None),
            P("seq", "chan", None),
        ),
        check_vma=False,
    )
```

profile of v0, /device:TPU:25, one launch (start us, length us, event | category | flops | bytes accessed | tf_op | source)
XLA Modules:
  0.0 245.6 jit_solution(8685788320649726147)
XLA Ops:
  7.2 0.0 copy-start
  7.2 0.9 copy.78
  8.1 5.8 %fusion.4 = bf16[10,384,512]{2,1,0:T(8,128)(2,1)} fusion(bf16[10,384,512]{2,1,0:T(8,128)(2,1)} %param.9, bf16[10,384,512]{2,1,0:T(8,128)(2,1)} %param.5), kind=kLoop, calls=%fused_computation.13 | loop fusion | flops 15728640 | bytes 11796480 | tf_op jit(solution)/shard_map/convert_element_type | solution.py:51
  13.9 6.3 %copy.64 = bf16[10,384,512]{1,2,0:T(8,128)(2,1)} copy(bf16[10,384,512]{2,1,0:T(8,128)(2,1)} %fusion.4) | data formatting | bytes 7864320 | tf_op jit(solution)/shard_map/convert_element_type | solution.py:51
  20.2 3.3 %convert_bitcast_fusion = bf16[10,384,8,64]{1,2,0,3:T(8,128)(2,1)S(1)} fusion(bf16[64,8,8,1]{2,1,3,0:T(8,128)(2,1)S(1)} %copy.78, bf16[10,384,512]{1,2,0:T(8,128)(2,1)} %copy.64), kind=kOutput, calls=%fused_computation.38 | convolution fusion | flops 33423360 | bytes 7872512 | tf_op jit(solution)/shard_map/cdkm,kim->cdik/dot_general | solution.py:54
  23.5 0.0 copy-start.4
  23.5 2.9 %copy.67 = bf16[10,384,8,64]{1,3,0,2:T(8,128)(2,1)} copy(bf16[10,384,8,64]{1,2,0,3:T(8,128)(2,1)S(1)} %convert_bitcast_fusion) | data formatting | bytes 7864320 | tf_op jit(solution)/shard_map/convert_element_type | solution.py:56
  26.4 5.1 %all-to-all-start.1 = ((bf16[10,384,8,64]{1,3,0,2:T(8,128)(2,1)}), bf16[10,384,8,64]{1,3,0,2:T(8,128)(2,1)}, u32[]{:S(2)}, u32[]{:S(2)}) async-start(bf16[10,384,8,64]{1,3,0,2:T(8,128)(2,1)} %copy.67), calls=%async_computation.1 | async-start | bytes 7864320 | tf_op jit(solution)/shard_map/all_to_all | solution.py:57
  31.5 1.5 slice.44
  33.1 0.4 copy.89
  33.5 3.7 %collective-permute-start = (bf16[10,384,3]{1,2,0:T(4,128)(2,1)S(1)}, bf16[10,384,3]{1,2,0:T(4,128)(2,1)S(1)}, u32[]{:S(2)}, u32[]{:S(2)}) collective-permute-start(bf16[10,384,3]{1,2,0:T(4,128)(2,1)S(1)} %copy.89), channel_id=1, source_target_pairs={{0,4},{4,8},{8,12},{12,16},{16,20},{20,24},{24,28},{1,5},{5,9},{9,... | collective-permute-start | bytes 69128 | tf_op jit(solution)/shard_map/ppermute | solution.py:12
  37.2 0.0 copy-done.4
  37.2 37.7 %collective-permute-done = bf16[10,384,3]{1,2,0:T(4,128)(2,1)S(1)} collective-permute-done((bf16[10,384,3]{1,2,0:T(4,128)(2,1)S(1)}, bf16[10,384,3]{1,2,0:T(4,128)(2,1)S(1)}, u32[]{:S(2)}, u32[]{:S(2)}) %collective-permute-start) | collective-permute-done | bytes 23072 | tf_op jit(solution)/shard_map/ppermute | solution.py:12
  74.9 0.5 copy.56
  75.4 4.3 %maximum_convert_fusion = f32[10,384,515]{2,1,0:T(8,128)S(1)} fusion(bf16[10,384,512]{2,1,0:T(8,128)(2,1)} %param.5, bf16[10,384,3]{2,1,0:T(8,128)(2,1)S(1)} %copy.56), kind=kLoop, calls=%fused_computation.37 | loop fusion | flops 7910400 | bytes 11865600 | tf_op jit(solution)/shard_map/convert_element_type | solution.py:32
  79.7 7.8 %fusion.18 = bf16[10,384,512]{2,1,0:T(8,128)(2,1)} fusion(f32[10,384,515]{2,1,0:T(8,128)S(1)} %maximum_convert_fusion, f32[384]{0:T(512)S(1)} %get-tuple-element.14, f32[384]{0:T(512)S(1)} %get-tuple-element.15, f32[384]{0:T(512)S(1)} %get-tuple-element.13, f32[384]{0:T(512)S(1)} %get-tuple-element.12), kind=kLoop, calls=%fused_computation.29 | loop fusion | flops 15728640 | bytes 35395584 | tf_op jit(solution)/shard_map/convert_element_type | solution.py:39
  87.5 0.0 copy-done
  87.5 6.2 %convert_bitcast_fusion.1 = bf16[10,384,1,512]{3,1,0,2:T(8,128)(2,1)} fusion(bf16[10,384,512]{2,1,0:T(8,128)(2,1)} %fusion.18, bf16[1,512,512]{2,1,0:T(8,128)(2,1)S(1)} %copy-done), kind=kOutput, calls=%fused_computation.39 | convolution fusion | flops 2015232000 | bytes 8388608 | tf_op jit(solution)/shard_map/cdij,ijk->cdik/dot_general | solution.py:40
  93.7 9.1 %copy.57 = bf16[10,384,1,512]{1,0,2,3:T(8,128)(2,1)} copy(bf16[10,384,1,512]{3,1,0,2:T(8,128)(2,1)} %convert_bitcast_fusion.1) | data formatting | bytes 7864320 | tf_op jit(solution)/shard_map/convert_element_type | solution.py:42
  102.9 0.0 all-to-all-done.1
  102.9 5.0 %all-to-all-start = ((bf16[10,384,1,512]{1,0,2,3:T(8,128)(2,1)}), bf16[10,384,1,512]{1,0,2,3:T(8,128)(2,1)}, u32[]{:S(2)}, u32[]{:S(2)}) async-start(bf16[10,384,1,512]{1,0,2,3:T(8,128)(2,1)} %copy.57), calls=%async_computation | async-start | bytes 12582912 | tf_op jit(solution)/shard_map/all_to_all | solution.py:43
  107.9 0.0 reduce-scatter.5.cloned.1.call-start
  107.9 0.0 copy-start.3
  107.9 2.7 %copy.68 = bf16[10,384,8,64]{1,3,2,0:T(8,128)(2,1)S(1)} copy(bf16[10,384,8,64]{1,3,0,2:T(8,128)(2,1)} %all-to-all-done.1) | data formatting | bytes 7864320 | tf_op jit(solution)/shard_map/all_to_all | solution.py:57
  110.7 0.0 copy-start.2
  110.7 1.9 copy-done.2
  112.6 0.0 copy-done.3
  112.6 3.2 %convolution_bitcast_fusion.1 = f32[1,512,512]{2,1,0:T(8,128)} fusion(bf16[10,384,512]{2,1,0:T(8,128)(2,1)S(1)} %copy-done.3, bf16[10,384,512]{1,2,0:T(8,128)(2,1)S(1)} %bitcast.45), kind=kOutput, calls=%fused_computation.47 | convolution fusion | flops 2013265920 | bytes 8912896 | tf_op jit(solution)/shard_map/cdij,cdik->ijk/dot_general | solution.py:58
  115.8 60.2 %all-to-all-done = bf16[10,384,1,512]{1,0,2,3:T(8,128)(2,1)} async-done(((bf16[10,384,1,512]{1,0,2,3:T(8,128)(2,1)}), bf16[10,384,1,512]{1,0,2,3:T(8,128)(2,1)}, u32[]{:S(2)}, u32[]{:S(2)}) %all-to-all-start) | async-done | bytes 3932192 | tf_op jit(solution)/shard_map/all_to_all | solution.py:43
  176.0 7.1 %fusion.29 = f32[64,8,8]{2,1,0:T(8,128)S(1)} fusion(bf16[10,384,8,64]{1,0,3,2:T(8,128)(2,1)} %bitcast.6, bf16[10,384,512]{1,2,0:T(8,128)(2,1)} %copy.64), kind=kOutput, calls=%fused_computation.48 | convolution fusion | flops 31457280 | bytes 7880704 | tf_op jit(solution)/shard_map/cdik,cdkm->kim/dot_general | solution.py:53
  183.2 0.8 copy.76
  183.9 0.0 reduce-scatter.5.cloned.1.call-update
  183.9 0.0 reduce-scatter.3.cloned.1.call-start
  184.0 4.4 %fusion.34 = f32[10,384,512]{2,1,0:T(8,128)S(1)} fusion(bf16[10,384,512]{1,2,0:T(8,128)(2,1)} %bitcast.46, bf16[1,512,512]{2,1,0:T(8,128)(2,1)S(1)} %copy-done), kind=kOutput, calls=%fused_computation.49 | convolution fusion | flops 2013265920 | bytes 12320768 | tf_op jit(solution)/shard_map/cdik,ijk->cdij/dot_general | solution.py:59
  188.4 0.0 copy-start.1
  188.4 3.1 %copy-done.1 = f32[10,384,512]{2,1,0:T(8,128)} copy-done((f32[10,384,512]{2,1,0:T(8,128)}, f32[10,384,512]{2,1,0:T(8,128)S(1)}, u32[]{:S(2)}) %copy-start.1) | copy-done | bytes 7864344
  191.5 0.3 slice.60
  191.8 0.6 copy.70
  192.4 5.7 %collective-permute-start.1 = (f32[10,384,3]{1,2,0:T(4,128)S(1)}, f32[10,384,3]{1,2,0:T(4,128)S(1)}, u32[]{:S(2)}, u32[]{:S(2)}) collective-permute-start(f32[10,384,3]{1,2,0:T(4,128)S(1)} %copy.70), channel_id=1, source_target_pairs={{4,0},{8,4},{12,8},{16,12},{20,16},{24,20},{28,24},{5,1},{9,5},{13... | collective-permute-start | bytes 138248 | tf_op jit(solution)/shard_map/ppermute | solution.py:12
  198.1 0.0 reduce-scatter.3.cloned.1.call-update
  198.1 5.2 %convolution_bitcast_fusion = f32[10,384,64,8]{1,3,0,2:T(8,128)S(1)} fusion(bf16[64,8,8,1]{2,1,3,0:T(8,128)(2,1)S(1)} %copy.78, bf16[10,384,8,64]{1,0,3,2:T(8,128)(2,1)} %bitcast.6), kind=kOutput, calls=%fused_computation.44 | convolution fusion | flops 31457280 | bytes 11804672 | tf_op jit(solution)/shard_map/cdik,kim->cdkm/dot_general | solution.py:44
  203.4 3.7 %copy.105 = f32[10,384,64,8]{1,3,2,0:T(8,128)} copy(f32[10,384,64,8]{1,3,0,2:T(8,128)S(1)} %convolution_bitcast_fusion) | data formatting | bytes 15728640 | tf_op jit(solution)/shard_map/cdik,kim->cdkm/transpose | solution.py:44
  207.1 9.1 %copy.62 = f32[10,384,512]{2,1,0:T(8,128)} copy(f32[10,384,512]{1,2,0:T(8,128)} %bitcast.44) | data formatting | bytes 15728640 | tf_op jit(solution)/shard_map/reshape | solution.py:46
  216.2 0.0 collective-permute-done.1
  216.2 0.6 copy.71
  216.8 21.9 %fusion.3 = (bf16[10,384,512]{2,1,0:T(8,128)(2,1)}, bf16[10,384,512]{2,1,0:T(8,128)(2,1)}) fusion(f32[10,384,512]{2,1,0:T(8,128)} %copy.62, bf16[10,384,512]{2,1,0:T(8,128)(2,1)} %param.9, f32[10,384,512]{2,1,0:T(8,128)} %copy-done.1, bf16[10,384,512]{2,1,0:T(8,128)(2,1)} %param.5, f32[10,384,3]{2,1,0:T(8,128)S(1)} %copy.71, f32[384]{0:T(512)S(1)} %get-tuple-element.14, ...), kind=kLoop, calls=%fused_computation.12 | loop fusion | flops 51118080 | bytes 31509504 | tf_op jit(solution)/shard_map/convert_element_type | solution.py:67
  238.7 0.0 reduce-scatter.5.cloned.1.call-done
  238.7 0.0 reduce-scatter.3.cloned.1.call-done
  (1 shorter events, 0.0 us)
Async XLA Ops:
  7.2 80.3 %copy-start = (bf16[1,512,512]{2,1,0:T(8,128)(2,1)S(1)}, bf16[1,512,512]{2,1,0:T(8,128)(2,1)}, u32[]{:S(2)}) copy-start(bf16[1,512,512]{2,1,0:T(8,128)(2,1)} %param.7) | copy-start | bytes 1572868
  23.5 13.7 %copy-start.4 = (f32[4,384]{1,0:T(4,128)S(1)}, f32[4,384]{1,0:T(4,128)}, u32[]{:S(2)}) copy-start(f32[4,384]{1,0:T(4,128)} %param.6) | copy-start | bytes 18436
  26.4 76.4 %all-to-all-start.1 = ((bf16[10,384,8,64]{1,3,0,2:T(8,128)(2,1)}), bf16[10,384,8,64]{1,3,0,2:T(8,128)(2,1)}, u32[]{:S(2)}, u32[]{:S(2)}) async-start(bf16[10,384,8,64]{1,3,0,2:T(8,128)(2,1)} %copy.67), calls=%async_computation.1 | async-start | bytes 7864320 | tf_op jit(solution)/shard_map/all_to_all | solution.py:57
  33.5 41.4 %collective-permute-start = (bf16[10,384,3]{1,2,0:T(4,128)(2,1)S(1)}, bf16[10,384,3]{1,2,0:T(4,128)(2,1)S(1)}, u32[]{:S(2)}, u32[]{:S(2)}) collective-permute-start(bf16[10,384,3]{1,2,0:T(4,128)(2,1)S(1)} %copy.89), channel_id=1, source_target_pairs={{0,4},{4,8},{8,12},{12,16},{16,20},{20,24},{24,28},{1,5},{5,9},{9,... | collective-permute-start | bytes 69128 | tf_op jit(solution)/shard_map/ppermute | solution.py:12
  102.9 73.2 %all-to-all-start = ((bf16[10,384,1,512]{1,0,2,3:T(8,128)(2,1)}), bf16[10,384,1,512]{1,0,2,3:T(8,128)(2,1)}, u32[]{:S(2)}, u32[]{:S(2)}) async-start(bf16[10,384,1,512]{1,0,2,3:T(8,128)(2,1)} %copy.57), calls=%async_computation | async-start | bytes 12582912 | tf_op jit(solution)/shard_map/all_to_all | solution.py:43
  107.9 130.8 %reduce-scatter.5.cloned.1.call-start = ((), (), s32[]{:S(2)}) async-start(), calls=%async_computation.5 | async-start | bytes 40960 | tf_op jit(solution)/shard_map/reduce_scatter | solution.py:18
  107.9 4.7 %copy-start.3 = (bf16[10,384,512]{2,1,0:T(8,128)(2,1)S(1)}, bf16[10,384,512]{2,1,0:T(8,128)(2,1)}, u32[]{:S(2)}) copy-start(bf16[10,384,512]{2,1,0:T(8,128)(2,1)} %fusion.18) | copy-start | bytes 11796484
  110.7 1.9 copy-start.2
  183.9 54.8 %reduce-scatter.3.cloned.1.call-start = ((), (), s32[]{:S(2)}) async-start(), calls=%async_computation.4 | async-start | bytes 1310720 | tf_op jit(solution)/shard_map/reduce_scatter | solution.py:17
  188.4 3.1 %copy-start.1 = (f32[10,384,512]{2,1,0:T(8,128)}, f32[10,384,512]{2,1,0:T(8,128)S(1)}, u32[]{:S(2)}) copy-start(f32[10,384,512]{2,1,0:T(8,128)S(1)} %fusion.34) | copy-start | bytes 23592964
  192.4 23.8 %collective-permute-start.1 = (f32[10,384,3]{1,2,0:T(4,128)S(1)}, f32[10,384,3]{1,2,0:T(4,128)S(1)}, u32[]{:S(2)}, u32[]{:S(2)}) collective-permute-start(f32[10,384,3]{1,2,0:T(4,128)S(1)} %copy.70), channel_id=1, source_target_pairs={{4,0},{8,4},{12,8},{16,12},{20,16},{24,20},{28,24},{5,1},{9,5},{13... | collective-permute-start | bytes 138248 | tf_op jit(solution)/shard_map/ppermute | solution.py:12
Sparse Core Ops, SparseCore 0:
  184.1 16.4 reduce-scatter.4
  203.6 27.4 reduce-scatter.2
where the time goes:
time: 246 us
  waiting for transfers between devices  97.9 us (40%)
  local copies, waits for them, and re-layouts  44.4 us (18%)
  other arithmetic  39.8 us (16%)
  matrix products  29.5 us (12%)
  starting transfers between devices  19.7 us (8%)
  between operations  14.2 us (6%)
    all_to_all x1, waiting for transfers between devices, shards(): lax.all_to_all(first, 'seq', split_axis=3, concat_axis=2, tiled=True)  60.2 us
    ppermute x2, waiting for transfers between devices, from_behind(): lax.ppermute(value, axis, [(source, source + steps) for source in range(l...  37.7 us
    convert_element_type x1, other arithmetic, shards(): frames_grad = (gate_part + conv_back).astype(jnp.bfloat16)  21.9 us
    ppermute x2, starting transfers between devices, from_behind(): lax.ppermute(value, axis, [(source, source + steps) for source in range(l...  9.46 us
    convert_element_type x1, local copies, waits for them, and re-layouts, shards(): first = jnp.einsum('cdij,ijk->cdik', conv, left_factor, preferred_element...  9.12 us
    reshape x1, local copies, waits for them, and re-layouts, shards(): second = jnp.einsum('cdik,kim->cdkm', columns, right_factor, preferred_el...  9.09 us
    convert_element_type x1, other arithmetic, shards(): mixed_conv.astype(jnp.bfloat16).reshape(clips, chans, blocks_here, width)  7.82 us
    dot_general x1, matrix products, shards(): jnp.einsum('cdik,cdkm->kim', columns, dsecond, preferred_element_type=jnp...  7.13 us
  transfers between devices with their start and end apart: 6, of which 2 were waited for; matrix products, arithmetic and copies ran while one was open for 33% of the time, Pallas kernels for 0%

commit v1 on v0

v1 whole, which is shorter than its diff:
```python
import functools

import jax
import jax.numpy as jnp
from jax import lax
from jax.experimental import pallas as pl
from jax.experimental.pallas import tpu as pltpu
from jax.sharding import PartitionSpec as P

TAPS = 4
LANES = 128
EDGE = 16
BACK = 8
LAG = 4
F32 = jnp.float32
BF16 = jnp.bfloat16
MESH = pl.DeviceIdType.MESH


def dot(a, b, ca, cb):
    return lax.dot_general(a, b, (((ca,), (cb,)), ((), ())), preferred_element_type=F32)


def block_kernel(
    nseq, nchan,
    frames_hbm, grad_hbm, taps_ref, left_ref, right_ref,
    mixed_hbm, fgrad_hbm, lgrad_ref, rgrad_ref,
    fr, og, sa, ra, sb, rb, conv, mix, fg, gp, work, dsec, left_t, wide, acc_r, acc_l,
    tapb, edge, edge_s, edge_r, back_s, back_r, lsend, lrecv, rsend, rrecv,
    in_sem, out_sem, a_send, a_recv, b_send, b_recv, edge_sem, back_send, back_recv, sum_sem,
):
    clips, chans, rows = fr.shape
    keep = rows // nseq
    inner = rows // keep
    part = rows // nchan
    step_rows = 32
    me = lax.axis_index("seq")
    z = lax.axis_index("chan")
    nxt = lax.rem(me + 1, nseq)
    prv = lax.rem(me + nseq - 1, nseq)
    mine = pl.ds(pl.multiple_of(me * keep, keep), keep)

    def load(c, which):
        source, held = ((frames_hbm, fr), (grad_hbm, og))[which]
        return pltpu.make_async_copy(source.at[c], held.at[c], in_sem.at[which, c])

    def store(c, which):
        held, target = ((mix, mixed_hbm), (fg, fgrad_hbm))[which]
        return pltpu.make_async_copy(held.at[c], target.at[c], out_sem.at[which, c])

    def remote(src, dst, send, recv, axis, to):
        return pltpu.make_async_remote_copy(
            src_ref=src, dst_ref=dst, send_sem=send, recv_sem=recv,
            device_id={axis: to}, device_id_type=MESH,
        )

    @pl.loop(0, clips)
    def _(c):
        load(c, 0).start()

    @pl.loop(0, clips)
    def _(c):
        load(c, 1).start()

    barrier = pltpu.get_barrier_semaphore()
    for p in range(1, nseq):
        pl.semaphore_signal(
            barrier, inc=1, device_id={"seq": lax.rem(me + p, nseq)}, device_id_type=MESH
        )
    for p in range(1, nchan):
        pl.semaphore_signal(
            barrier, inc=1, device_id={"chan": lax.rem(z + p, nchan)}, device_id_type=MESH
        )

    pick = (
        lax.broadcasted_iota(jnp.int32, (EDGE, LANES), 1)
        == lax.broadcasted_iota(jnp.int32, (EDGE, LANES), 0) + (LANES - EDGE)
    )
    pick_in = jnp.where(pick, 1.0, 0.0).astype(BF16)

    @pl.loop(0, clips)
    def _(c):
        load(c, 0).wait()
        edge_s[c] = dot(pick_in, fr[c, :, rows - LANES :], 1, 1).astype(BF16)

    pl.semaphore_wait(barrier, nseq + nchan - 2)
    edge_copy = remote(edge_s, edge_r, edge_sem.at[0], edge_sem.at[1], "seq", nxt)
    edge_copy.start()

    left_t[...] = left_ref[...].astype(F32).T.astype(BF16)
    for k in range(TAPS):
        tapb[k] = jnp.broadcast_to(taps_ref[:, k : k + 1], (chans, LANES))
    spread = (
        lax.rem(lax.broadcasted_iota(jnp.int32, (inner, rows), 1), inner)
        == lax.broadcasted_iota(jnp.int32, (inner, rows), 0)
    )
    spread = jnp.where(spread, 1.0, 0.0).astype(BF16)
    own_k = (
        lax.rem(lax.broadcasted_iota(jnp.int32, (rows, rows), 0), keep)
        == lax.broadcasted_iota(jnp.int32, (rows, rows), 1) // inner
    )
    wide[...] = jnp.where(own_k, dot(right_ref[...], spread, 1, 0), 0.0).astype(BF16)
    acc_r[...] = jnp.zeros_like(acc_r)
    acc_l[...] = jnp.zeros_like(acc_l)
    pick_prev = jnp.where(jnp.logical_and(pick, me > 0), 1.0, 0.0).astype(BF16)
    pick_next = (
        lax.broadcasted_iota(jnp.int32, (2 * BACK, LANES), 1)
        == lax.rem(lax.broadcasted_iota(jnp.int32, (2 * BACK, LANES), 0), BACK)
    )
    pick_next = jnp.where(jnp.logical_and(pick_next, me < nseq - 1), 1.0, 0.0).astype(BF16)
    edge_copy.wait()

    def tap(k, at):
        return jnp.concatenate([tapb[k, at, :]] * (rows // LANES), axis=1)

    def chunks(body):
        @pl.loop(0, chans // step_rows)
        def _(r):
            body(pl.ds(pl.multiple_of(r * step_rows, step_rows), step_rows))

    def scatter(c, src, dst, send, recv):
        @pl.loop(1, nseq)
        def _(p):
            to = lax.rem(me + p, nseq)
            there = pl.ds(pl.multiple_of(to * keep, keep), keep)
            remote(src.at[c, there], dst.at[c, mine], send.at[c], recv.at[c], "seq", to).start()

    def arrivals(c, src, dst, send, recv):
        others = pl.ds(0, (nseq - 1) * keep)
        return remote(src.at[c, others], dst.at[c, others], send.at[c], recv.at[c], "seq", nxt)

    @pl.loop(0, clips)
    def _(c):
        edge[...] = dot(edge_r[c], pick_prev, 0, 0)

        def body(at):
            x = jnp.concatenate([edge[at, :], fr[c, at, :].astype(F32)], axis=1)
            total = tap(0, at) * x[:, LANES:]
            for k in range(1, TAPS):
                total = total + tap(k, at) * pltpu.roll(x, k, 1)[:, LANES:]
            conv[c, at, :] = total.astype(BF16)

        chunks(body)
        sa[c] = dot(left_t[...], conv[c], 1, 1).astype(BF16)
        scatter(c, sa, ra, a_send, a_recv)
        ra[c, mine, :] = sa[c, mine, :]

    def forward(c):
        load(c, 1).wait()
        arrivals(c, sa, ra, a_send, a_recv).wait_recv()
        work[...] = dot(ra[c], wide[...], 0, 0)

        def body(at):
            x = fr[c, at, :].astype(F32)
            g = og[c, at, :].astype(F32)
            second = work[at, :]
            sig = jax.nn.sigmoid(x)
            gate = x * sig
            mix[c, at, :] = (second * gate).astype(BF16)
            dsec[at, :] = (g * gate).astype(BF16)
            gp[c, at, :] = g * second * sig * (1.0 + x * (1.0 - sig))

        chunks(body)
        sb[c] = dot(wide[...], dsec[...], 1, 1).astype(BF16)
        scatter(c, sb, rb, b_send, b_recv)
        rb[c, mine, :] = sb[c, mine, :]
        acc_r[...] += dot(ra[c], dsec[...], 1, 0)
        store(c, 0).start()

    def sum_right(p):
        to = lax.rem(z + p, nchan)
        there = pl.ds(pl.multiple_of(to * part, part), part)
        return remote(
            rsend.at[there], rrecv.at[p - 1], sum_sem.at[0, p - 1], sum_sem.at[1, p - 1], "chan", to
        )

    def sum_left(p):
        to = lax.rem(z + p, nchan)
        there = pl.ds(pl.multiple_of(to * part, part), part)
        return remote(
            lsend.at[there], lrecv.at[p - 1], sum_sem.at[2, p - 1], sum_sem.at[3, p - 1], "chan", to
        )

    def send_right():
        own = jnp.where(own_k, acc_r[...], 0.0)
        fold = (
            lax.rem(lax.broadcasted_iota(jnp.int32, (rows, LANES), 0), inner)
            == lax.broadcasted_iota(jnp.int32, (rows, LANES), 1)
        )
        fold = jnp.where(fold, 1.0, 0.0).astype(BF16)
        high = own.astype(BF16)
        rest = own - high.astype(F32)
        mid = rest.astype(BF16)
        low = (rest - mid.astype(F32)).astype(BF16)
        rsend[...] = dot(high, fold, 1, 0) + dot(mid, fold, 1, 0) + dot(low, fold, 1, 0)
        for p in range(1, nchan):
            sum_right(p).start()

    def back_edge(c):
        return remote(back_s.at[c], back_r.at[c], back_send.at[c], back_recv.at[c], "seq", prv)

    def backward(c):
        arrivals(c, sb, rb, b_send, b_recv).wait_recv()
        back_s[c] = dot(left_ref[:EDGE, :], rb[c], 1, 0)[:BACK]
        back_edge(c).start()
        acc_l[...] += dot(rb[c], conv[c], 1, 0)

    def send_left():
        acc_r[...] = acc_l[...].T
        lsend[...] = acc_r[...].astype(BF16)
        for p in range(1, nchan):
            sum_left(p).start()

    def finish(c):
        work[...] = dot(rb[c], left_t[...], 0, 0)
        back_edge(c).wait_recv()
        value = back_r[c]
        high = value.astype(BF16).astype(F32)
        both = jnp.concatenate([high, value - high], axis=0).astype(BF16)
        edge[...] = dot(both, pick_next, 0, 0)

        def body(at):
            d = jnp.concatenate([work[at, :], edge[at, :]], axis=1)
            total = gp[c, at, :] + tap(0, at) * d[:, :rows]
            for k in range(1, TAPS):
                total = total + tap(k, at) * pltpu.roll(d, rows + LANES - k, 1)[:, :rows]
            fg[c, at, :] = total.astype(BF16)

        chunks(body)
        store(c, 1).start()

    @pl.loop(0, clips + LAG + 1)
    def _(t):
        pl.when(t < clips)(lambda: forward(t))
        pl.when(t == clips)(send_right)
        pl.when(jnp.logical_and(t >= LAG, t < clips + LAG))(lambda: backward(t - LAG))
        pl.when(t == clips + LAG - 1)(send_left)
        pl.when(t > LAG)(lambda: finish(t - LAG - 1))

    here = pl.ds(pl.multiple_of(z * part, part), part)
    right_total = rsend[here, :]
    for p in range(1, nchan):
        sum_right(p).wait()
        right_total = right_total + rrecv[p - 1]
    rgrad_ref[...] = right_total
    left_total = acc_r[here, :]
    for p in range(1, nchan):
        sum_left(p).wait()
        left_total = left_total + lrecv[p - 1].astype(F32)
    lgrad_ref[...] = left_total

    @pl.loop(0, clips)
    def _(c):
        arrivals(c, sa, ra, a_send, a_recv).wait_send()
        arrivals(c, sb, rb, b_send, b_recv).wait_send()
        back_edge(c).wait_send()
        store(c, 0).wait()
        store(c, 1).wait()


def shards(nseq, nchan, frames, conv_taps, left_factor, right_factor, out_grad):
    clips, chans, rows = frames.shape
    keep, inner = right_factor.shape[0], right_factor.shape[1]
    part = rows // nchan
    slabs = (clips, rows, chans)
    slots = max(nchan - 1, 1)
    right_rows = jnp.swapaxes(right_factor, 0, 1).reshape(inner * keep, inner)
    vmem = pl.BlockSpec(memory_space=pltpu.VMEM)
    anywhere = pl.BlockSpec(memory_space=pl.ANY)
    dma = pltpu.SemaphoreType.DMA
    mixed, frames_grad, left_grad, right_grad = pl.pallas_call(
        functools.partial(block_kernel, nseq, nchan),
        out_shape=(
            jax.ShapeDtypeStruct(frames.shape, BF16),
            jax.ShapeDtypeStruct(frames.shape, BF16),
            jax.ShapeDtypeStruct((part, rows), F32),
            jax.ShapeDtypeStruct((part, LANES), F32),
        ),
        in_specs=[anywhere, anywhere, vmem, vmem, vmem],
        out_specs=(anywhere, anywhere, vmem, vmem),
        scratch_shapes=[
            pltpu.VMEM(frames.shape, BF16),
            pltpu.VMEM(frames.shape, BF16),
            pltpu.VMEM(slabs, BF16),
            pltpu.VMEM(slabs, BF16),
            pltpu.VMEM(slabs, BF16),
            pltpu.VMEM(slabs, BF16),
            pltpu.VMEM(frames.shape, BF16),
            pltpu.VMEM(frames.shape, BF16),
            pltpu.VMEM(frames.shape, BF16),
            pltpu.VMEM(frames.shape, F32),
            pltpu.VMEM((chans, rows), F32),
            pltpu.VMEM((chans, rows), BF16),
            pltpu.VMEM((rows, rows), BF16),
            pltpu.VMEM((rows, rows), BF16),
            pltpu.VMEM((rows, rows), F32),
            pltpu.VMEM((rows, rows), F32),
            pltpu.VMEM((TAPS, chans, LANES), F32),
            pltpu.VMEM((chans, LANES), F32),
            pltpu.VMEM((clips, EDGE, chans), BF16),
            pltpu.VMEM((clips, EDGE, chans), BF16),
            pltpu.VMEM((clips, BACK, chans), F32),
            pltpu.VMEM((clips, BACK, chans), F32),
            pltpu.VMEM((rows, rows), BF16),
            pltpu.VMEM((slots, part, rows), BF16),
            pltpu.VMEM((rows, LANES), F32),
            pltpu.VMEM((slots, part, LANES), F32),
            dma((2, clips)),
            dma((2, clips)),
            dma((clips,)),
            dma((clips,)),
            dma((clips,)),
            dma((clips,)),
            dma((2,)),
            dma((clips,)),
            dma((clips,)),
            dma((4, slots)),
        ],
        compiler_params=pltpu.CompilerParams(
            collective_id=0, has_side_effects=True, vmem_limit_bytes=60 * 2**20
        ),
    )(frames, out_grad, conv_taps.T, left_factor[0], right_rows)
    right_grad = jnp.swapaxes(right_grad[:, :inner].reshape(-1, keep, inner), 0, 1)
    return mixed, frames_grad, left_grad[None], right_grad


def solution(mesh):
    placed = (
        P(None, "chan", "seq"),
        P(None, "chan"),
        P("seq", None, None),
        P("seq", None, None),
        P(None, "chan", "seq"),
    )
    return jax.shard_map(
        functools.partial(shards, mesh.shape["seq"], mesh.shape["chan"]),
        mesh=mesh,
        in_specs=placed,
        out_specs=(
            P(None, "chan", "seq"),
            P(None, "chan", "seq"),
            P("seq", "chan", None),
            P("seq", "chan", None),
        ),
        check_vma=False,
    )
```

time: 246 us -> 133 us (0.54)
  Pallas kernels: 0 us -> 119 us
  waiting for transfers between devices: 97.9 us -> 0 us
  other arithmetic: 39.8 us -> 0 us
  local copies, waits for them, and re-layouts: 44.4 us -> 11.6 us
  matrix products: 29.5 us -> 0 us
  starting transfers between devices: 19.7 us -> 0 us
  between operations: 14.2 us -> 0.64 us
    pallas_call x0 -> x1, Pallas kernels: none -> 119 us  [shards(): pl.pallas_call(functools.partial(block_kernel, nseq, nchan), out_shape=(j...]
    all_to_all x2 -> x0, waiting for transfers between devices: 60.2 us -> none  [the longest x1 60.2 us: shards(): lax.all_to_all(first, 'seq', split_axis=3, concat_axis=2, tiled=True)]
    convert_element_type x4 -> x0, other arithmetic: 39.8 us -> none  [the longest x1 21.9 us: shards(): frames_grad = (gate_part + conv_back).astype(jnp.bfloat16)]
    ppermute x2 -> x0, waiting for transfers between devices: 37.7 us -> none  [from_behind(): lax.ppermute(value, axis, [(source, source + steps) for source in range(l...]
    dot_general x6 -> x0, matrix products: 29.5 us -> none  [the longest x1 7.13 us: shards(): jnp.einsum('cdik,cdkm->kim', columns, dsecond, preferred_element_type=jnp...]
    convert_element_type x3 -> x0, local copies, waits for them, and re-layouts: 18.3 us -> none  [the longest x1 9.12 us: shards(): first = jnp.einsum('cdij,ijk->cdik', conv, left_factor, preferred_element...]
    all_to_all x2 -> x0, starting transfers between devices: 10.1 us -> none  [the longest x1 5.11 us: shards(): lax.all_to_all(dfirst, 'seq', split_axis=2, concat_axis=3, tiled=True)]
    ppermute x2 -> x0, starting transfers between devices: 9.46 us -> none  [from_behind(): lax.ppermute(value, axis, [(source, source + steps) for source in range(l...]
  transfers between devices with their start and end apart: 6 -> 0, of which waited for: 2 -> 0; matrix products, arithmetic and copies ran while one was open for 33% -> 0% of each run, Pallas kernels for 0% -> 0%
where the time goes in v1:
time: 133 us; the launch traced here: 131 us
  Pallas kernels  119 us (89%)
  local copies, waits for them, and re-layouts  11.6 us (9%)
    pallas_call x1, Pallas kernels, shards(): pl.pallas_call(functools.partial(block_kernel, nseq, nchan), out_shape=(j...  119 us
    unnamed x8, local copies, waits for them, and re-layouts  8.6 us

profile of v1, /device:TPU:25, one launch (start us, length us, event | category | flops | bytes accessed | tf_op | source)
XLA Modules:
  0.0 131.1 jit_solution(14508192493969033500)
XLA Ops:
  0.6 1.5 %copy.10 = bf16[8,64,8]{2,1,0:T(8,128)(2,1)} copy(bf16[8,64,8]{1,2,0:T(8,128)(2,1)} %bitcast.13) | data formatting | bytes 16384 | tf_op jit(solution)/shard_map/transpose | solution.py:267
  2.1 1.5 %copy.9 = f32[4,384]{0,1:T(8,128)} copy(f32[4,384]{1,0:T(4,128)} %param.6) | data formatting | bytes 12288 | tf_op args[1]
  3.6 118.9 %shard_map.84 = (bf16[10,384,512]{2,1,0:T(8,128)(2,1)}, bf16[10,384,512]{2,1,0:T(8,128)(2,1)}, f32[128,512]{1,0:T(8,128)}, f32[128,128]{1,0:T(8,128)}) custom-call(bf16[10,384,512]{2,1,0:T(8,128)(2,1)} %frames_hbm.1, bf16[10,384,512]{2,1,0:T(8,128)(2,1)} %grad_hbm.1, f32[384,4]{1,0:T(8,128)} %bitcast.8, bf16[512,512]{1,0:T(8,128)(2,1)} %bitcast.10, ...), custom_call_target="tpu_custom_call" | custom-call | tf_op jit(solution)/shard_map/pallas_call | solution.py:271
  122.5 1.5 %copy.11 = f32[2,64,8]{1,2,0:T(8,128)} copy(f32[2,64,8]{2,1,0:T(8,128)} %bitcast.12) | data formatting | bytes 8192 | tf_op jit(solution)/shard_map/reshape | solution.py:323
  124.0 0.0 copy-start
  124.0 4.5 %copy.15 = bf16[10,384,512]{2,1,0:T(8,128)(2,1)} copy(bf16[10,384,512]{2,1,0:T(8,128)(2,1)} %get-tuple-element.16) | data formatting | bytes 7864320
  128.5 0.0 copy-done
  128.5 0.0 copy-start.1
  128.5 1.9 %copy.16 = bf16[10,384,512]{2,1,0:T(8,128)(2,1)} copy(bf16[10,384,512]{2,1,0:T(8,128)(2,1)S(1)} %copy-done) | data formatting | bytes 7864320
  130.4 0.0 copy-done.1
  130.4 0.7 copy.17
Async XLA Ops:
  124.0 4.5 %copy-start = (bf16[10,384,512]{2,1,0:T(8,128)(2,1)S(1)}, bf16[10,384,512]{2,1,0:T(8,128)(2,1)}, u32[]{:S(2)}) copy-start(bf16[10,384,512]{2,1,0:T(8,128)(2,1)} %get-tuple-element.17) | copy-start | bytes 11796484
  128.5 1.9 %copy-start.1 = (f32[128,512]{1,0:T(8,128)S(1)}, f32[128,512]{1,0:T(8,128)}, u32[]{:S(2)}) copy-start(f32[128,512]{1,0:T(8,128)} %get-tuple-element.10) | copy-start | bytes 786436

commit v2 on v1

--- a/solution.py
+++ b/solution.py
@@ -12,6 +12,7 @@
 EDGE = 16
 BACK = 8
 LAG = 4
+TAIL = 4
 F32 = jnp.float32
 BF16 = jnp.bfloat16
 MESH = pl.DeviceIdType.MESH
@@ -89,19 +90,7 @@
 
     left_t[...] = left_ref[...].astype(F32).T.astype(BF16)
     for k in range(TAPS):
-        tapb[k] = jnp.broadcast_to(taps_ref[:, k : k + 1], (chans, LANES))
-    spread = (
-        lax.rem(lax.broadcasted_iota(jnp.int32, (inner, rows), 1), inner)
-        == lax.broadcasted_iota(jnp.int32, (inner, rows), 0)
-    )
-    spread = jnp.where(spread, 1.0, 0.0).astype(BF16)
-    own_k = (
-        lax.rem(lax.broadcasted_iota(jnp.int32, (rows, rows), 0), keep)
-        == lax.broadcasted_iota(jnp.int32, (rows, rows), 1) // inner
-    )
-    wide[...] = jnp.where(own_k, dot(right_ref[...], spread, 1, 0), 0.0).astype(BF16)
-    acc_r[...] = jnp.zeros_like(acc_r)
-    acc_l[...] = jnp.zeros_like(acc_l)
+        tapb[k] = jnp.broadcast_to(taps_ref[k : k + 1, :], (LANES, chans)).T
     pick_prev = jnp.where(jnp.logical_and(pick, me > 0), 1.0, 0.0).astype(BF16)
     pick_next = (
         lax.broadcasted_iota(jnp.int32, (2 * BACK, LANES), 1)
@@ -114,9 +103,13 @@
         return jnp.concatenate([tapb[k, at, :]] * (rows // LANES), axis=1)
 
     def chunks(body):
-        @pl.loop(0, chans // step_rows)
+        steps = chans // step_rows
+        group = max(g for g in (1, 2, 3, 4) if steps % g == 0)
+
+        @pl.loop(0, steps // group)
         def _(r):
-            body(pl.ds(pl.multiple_of(r * step_rows, step_rows), step_rows))
+            for g in range(group):
+                body(pl.ds(pl.multiple_of((r * group + g) * step_rows, step_rows), step_rows))
 
     def scatter(c, src, dst, send, recv):
         @pl.loop(1, nseq)
@@ -144,6 +137,25 @@
         sa[c] = dot(left_t[...], conv[c], 1, 1).astype(BF16)
         scatter(c, sa, ra, a_send, a_recv)
         ra[c, mine, :] = sa[c, mine, :]
+
+    own_k = (
+        lax.rem(lax.broadcasted_iota(jnp.int32, (rows, rows), 0), keep)
+        == lax.broadcasted_iota(jnp.int32, (rows, rows), 1) // inner
+    )
+    acc_r[...] = jnp.zeros_like(acc_r)
+    acc_l[...] = jnp.zeros_like(acc_l)
+    here_k = (
+        lax.broadcasted_iota(jnp.int32, (keep, rows), 0)
+        == lax.broadcasted_iota(jnp.int32, (keep, rows), 1) // inner
+    )
+    pair = lax.broadcasted_iota(jnp.int32, (inner * inner, rows), 0)
+    column = lax.rem(lax.broadcasted_iota(jnp.int32, (inner * inner, rows), 1), inner)
+
+    @pl.loop(0, inner)
+    def _(i):
+        choose = jnp.where(pair == column + i * inner, 1.0, 0.0).astype(BF16)
+        block = jnp.where(here_k, dot(right_ref[...], choose, 0, 0), 0.0).astype(BF16)
+        wide[pl.ds(pl.multiple_of(i * keep, keep), keep), :] = block
 
     def forward(c):
         load(c, 1).wait()
@@ -229,13 +241,13 @@
         chunks(body)
         store(c, 1).start()
 
-    @pl.loop(0, clips + LAG + 1)
+    @pl.loop(0, clips + LAG + TAIL)
     def _(t):
         pl.when(t < clips)(lambda: forward(t))
         pl.when(t == clips)(send_right)
         pl.when(jnp.logical_and(t >= LAG, t < clips + LAG))(lambda: backward(t - LAG))
         pl.when(t == clips + LAG - 1)(send_left)
-        pl.when(t > LAG)(lambda: finish(t - LAG - 1))
+        pl.when(t >= LAG + TAIL)(lambda: finish(t - LAG - TAIL))
 
     here = pl.ds(pl.multiple_of(z * part, part), part)
     right_total = rsend[here, :]
@@ -264,7 +276,7 @@
     part = rows // nchan
     slabs = (clips, rows, chans)
     slots = max(nchan - 1, 1)
-    right_rows = jnp.swapaxes(right_factor, 0, 1).reshape(inner * keep, inner)
+    right_rows = jnp.transpose(right_factor, (1, 2, 0)).reshape(inner * inner, keep)
     vmem = pl.BlockSpec(memory_space=pltpu.VMEM)
     anywhere = pl.BlockSpec(memory_space=pl.ANY)
     dma = pltpu.SemaphoreType.DMA
@@ -319,7 +331,7 @@
         compiler_params=pltpu.CompilerParams(
             collective_id=0, has_side_effects=True, vmem_limit_bytes=60 * 2**20
         ),
-    )(frames, out_grad, conv_taps.T, left_factor[0], right_rows)
+    )(frames, out_grad, conv_taps, left_factor[0], right_rows)
     right_grad = jnp.swapaxes(right_grad[:, :inner].reshape(-1, keep, inner), 0, 1)
     return mixed, frames_grad, left_grad[None], right_grad
 

time: 133 us -> 121 us (0.910)
  Pallas kernels: 119 us -> 110 us
  local copies, waits for them, and re-layouts: 11.6 us -> 8.59 us
    pallas_call x1, Pallas kernels: 119 us -> 110 us  [shards(): pl.pallas_call(functools.partial(block_kernel, nseq, nchan), out_shape=(j...]
    unnamed x8 -> x7, local copies, waits for them, and re-layouts: 8.6 us -> 7.09 us
    transpose x1 -> x0, local copies, waits for them, and re-layouts: 1.48 us -> none  [shards(): right_rows = jnp.swapaxes(right_factor, 0, 1).reshape(inner * keep, inner)]
where the time goes in v2:
time: 121 us; the launch traced here: 119 us
  Pallas kernels  110 us (91%)
  local copies, waits for them, and re-layouts  8.59 us (7%)
    pallas_call x1, Pallas kernels, shards(): pl.pallas_call(functools.partial(block_kernel, nseq, nchan), out_shape=(j...  110 us
    unnamed x7, local copies, waits for them, and re-layouts  7.09 us

profile of v2, /device:TPU:25, one launch (start us, length us, event | category | flops | bytes accessed | tf_op | source)
XLA Modules:
  0.0 119.1 jit_solution(10782252087042664845)
XLA Ops:
  0.6 109.9 %shard_map.84 = (bf16[10,384,512]{2,1,0:T(8,128)(2,1)}, bf16[10,384,512]{2,1,0:T(8,128)(2,1)}, f32[128,512]{1,0:T(8,128)}, f32[128,128]{1,0:T(8,128)}) custom-call(bf16[10,384,512]{2,1,0:T(8,128)(2,1)} %frames_hbm.1, bf16[10,384,512]{2,1,0:T(8,128)(2,1)} %grad_hbm.1, f32[4,384]{1,0:T(4,128)} %taps_ref.1, bf16[512,512]{1,0:T(8,128)(2,1)} %bitcast.8, ...), custom_call_target="tpu_custom_call" | custom-call | tf_op jit(solution)/shard_map/pallas_call | solution.py:283
  110.5 1.5 %copy.9 = f32[2,64,8]{1,2,0:T(8,128)} copy(f32[2,64,8]{2,1,0:T(8,128)} %bitcast.10) | data formatting | bytes 8192 | tf_op jit(solution)/shard_map/reshape | solution.py:335
  112.0 0.0 copy-start
  112.0 4.5 %copy.13 = bf16[10,384,512]{2,1,0:T(8,128)(2,1)} copy(bf16[10,384,512]{2,1,0:T(8,128)(2,1)} %get-tuple-element.16) | data formatting | bytes 7864320
  116.5 0.0 copy-done
  116.5 0.0 copy-start.1
  116.5 1.9 %copy.14 = bf16[10,384,512]{2,1,0:T(8,128)(2,1)} copy(bf16[10,384,512]{2,1,0:T(8,128)(2,1)S(1)} %copy-done) | data formatting | bytes 7864320
  118.4 0.0 copy-done.1
  118.4 0.7 copy.15
Async XLA Ops:
  112.0 4.5 %copy-start = (bf16[10,384,512]{2,1,0:T(8,128)(2,1)S(1)}, bf16[10,384,512]{2,1,0:T(8,128)(2,1)}, u32[]{:S(2)}) copy-start(bf16[10,384,512]{2,1,0:T(8,128)(2,1)} %get-tuple-element.17) | copy-start | bytes 11796484
  116.5 1.9 %copy-start.1 = (f32[128,512]{1,0:T(8,128)S(1)}, f32[128,512]{1,0:T(8,128)}, u32[]{:S(2)}) copy-start(f32[128,512]{1,0:T(8,128)} %get-tuple-element.10) | copy-start | bytes 786436
